TPU v7x, 128 devices: a whole 4x4x4 slice. The times are simulated.
128 devices in a mesh: blk: 4 (over x_hi, core), batch: 32 (over x_lo, y, z).
Axes of the slice: x: 4 (x_hi: 2, x_lo: 2; x = x_hi * 2 + x_lo), y: 4, z: 4, core: 2. Of those that a mesh axis runs over, the one named last changes fastest.
Arguments:
- pixels: bfloat16 [32, 1024, 768], P('batch', 'blk'), may hold values from -6 to 6
- positions: bfloat16 [32, 1024, 1024], P('batch', 'blk'), may hold values from -4 to 4
- segments: int32 [32, 1024], P('batch'), may hold values from -1 to 2, as said below
- groups: int32 [32, 1024], P('batch', 'blk'), may hold values from 0 to 3, as said below
- cotangent: bfloat16 [32, 1024, 1024], P('batch', 'blk'), may hold values from -6 to 6
- emb_weight: bfloat16 [4, 768, 1024], replicated, may hold values from -0.21875 to 0.21875
- emb_bias: float32 [4, 1024], replicated, may hold values from -2 to 2
- norm1_gain: float32 [1024], replicated, may hold values from 0.5 to 1.5
- norm1_bias: float32 [1024], replicated, may hold values from -2 to 2
- qkv_weight: bfloat16 [1024, 3072], replicated, may hold values from -0.1875 to 0.1875
- query_bias: float32 [1024], replicated, may hold values from -3 to 3
- value_bias: float32 [1024], replicated, may hold values from -0.3 to 0.3
- out_weight: bfloat16 [1024, 1024], replicated, may hold values from -3.5 to 3.5
- out_bias: float32 [1024], replicated, may hold values from -2 to 2
- norm2_gain: float32 [1024], replicated, may hold values from 0.5 to 1.5
- norm2_bias: float32 [1024], replicated, may hold values from -2 to 2
- fc1_weight: bfloat16 [1024, 4096], replicated, may hold values from -0.1875 to 0.1875
- fc1_bias: float32 [4096], replicated, may hold values from -2 to 2
- fc2_weight: bfloat16 [4096, 1024], replicated, may hold values from -0.09375 to 0.09375
- fc2_bias: float32 [1024], replicated, may hold values from -2 to 2
Outputs:
- block_out: bfloat16 [32, 1024, 1024], P('batch', 'blk')
- pixel_grad: bfloat16 [32, 1024, 768], P('batch', 'blk')
- grad_emb_weight: float32 [4, 768, 1024], P(None, None, ('blk', 'batch'))
- grad_emb_bias: float32 [4, 1024], P(None, ('blk', 'batch'))
- grad_norm1_gain: float32 [1024], P(('blk', 'batch'))
- grad_norm1_bias: float32 [1024], P(('blk', 'batch'))
- grad_qkv_weight: float32 [1024, 3072], P(('blk', 'batch'))
- grad_query_bias: float32 [1024], P(('blk', 'batch'))
- grad_value_bias: float32 [1024], P(('blk', 'batch'))
- grad_out_weight: float32 [1024, 1024], P(('blk', 'batch'))
- grad_out_bias: float32 [1024], P(('blk', 'batch'))
- grad_norm2_gain: float32 [1024], P(('blk', 'batch'))
- grad_norm2_bias: float32 [1024], P(('blk', 'batch'))
- grad_fc1_weight: float32 [1024, 4096], P(('blk', 'batch'))
- grad_fc1_bias: float32 [4096], P(('blk', 'batch'))
- grad_fc2_weight: float32 [4096, 1024], P(('blk', 'batch'))
- grad_fc2_bias: float32 [1024], P(('blk', 'batch'))
Inputs may be any that keep to these rules, and one draw needn't show every extreme that they name: `segments`: items are contiguous runs of slots numbered 0, 1, 2 in order along the row; a run of 196 slots is an RGB item, one of 588 slots a 13-band item; every other slot is padding (-1). `groups`: 3 on RGB items; the three runs of 196 slots of a 13-band item hold groups 0, 1 and 2 in some order; on padding any group.
All inputs are finite; a program needn't handle non-finite values.
Results may differ from a plain program's by a relative error of at most 0.015.
Values may be sent and summed in bfloat16 or wider, within the bound.
A program may use at most 256 MiB of HBM per device.

v0:
```python
from functools import partial

import jax
import jax.numpy as jnp
from jax import lax
from jax.sharding import PartitionSpec as P

HD = 64


NORM_EPS = 1e-06
MASKED = -1e30


def normalize(values):
    center = values - jnp.mean(values, axis=-1, keepdims=True)
    spread = jnp.mean(center * center, axis=-1, keepdims=True)
    return center * lax.rsqrt(spread + NORM_EPS)


def norm_apply(values, gain, shift):
    return normalize(values) * gain + shift


def on_device(
    pixels,
    positions,
    segments,
    groups,
    cotangent,
    emb_weight,
    emb_bias,
    norm1_gain,
    norm1_bias,
    qkv_weight,
    query_bias,
    value_bias,
    out_weight,
    out_bias,
    norm2_gain,
    norm2_bias,
    fc1_weight,
    fc1_bias,
    fc2_weight,
    fc2_bias,
):
    rows_dev, slice_len, pix_len = pixels.shape
    model_width = qkv_weight.shape[0]
    head_count = model_width // HD
    band_count = emb_weight.shape[0]
    tok_count = rows_dev * slice_len
    score_scale = HD ** (-0.5)
    offset = lax.axis_index("blk") * slice_len
    query_seg = lax.dynamic_slice_in_dim(segments, offset, slice_len, 1)
    live_mask = (query_seg >= 0).astype(jnp.float32).reshape(tok_count, 1)
    allowed = query_seg[:, None, :, None] == segments[:, None, None, :]
    flat_pixels = pixels.reshape(tok_count, pix_len)
    band_hot = (
        groups.reshape(tok_count, 1) == jnp.arange(band_count, dtype=jnp.int32)[None, :]
    ).astype(jnp.float32)
    embedded = positions.reshape(tok_count, model_width).astype(jnp.float32)
    embedded = embedded + jnp.dot(band_hot, emb_bias, precision=lax.Precision.HIGHEST)
    for band_index in range(band_count):
        embedded = embedded + band_hot[:, band_index : band_index + 1] * jnp.dot(
            flat_pixels, emb_weight[band_index], preferred_element_type=jnp.float32
        )
    normed_one = norm_apply(embedded, norm1_gain, norm1_bias).astype(jnp.bfloat16)
    packed = jnp.dot(normed_one, qkv_weight, preferred_element_type=jnp.float32)
    query = (
        (packed[:, :model_width] + query_bias)
        .astype(jnp.bfloat16)
        .reshape(rows_dev, slice_len, head_count, HD)
    )
    keys = (
        packed[:, model_width : 2 * model_width]
        .astype(jnp.bfloat16)
        .reshape(rows_dev, slice_len, model_width)
    )
    values = (
        (packed[:, 2 * model_width :] + value_bias)
        .astype(jnp.bfloat16)
        .reshape(rows_dev, slice_len, model_width)
    )

    def score_block(key_piece):
        key_heads = key_piece.reshape(rows_dev, key_piece.shape[1], head_count, HD)
        raw = (
            jnp.einsum("rqhd,rkhd->rhqk", query, key_heads, preferred_element_type=jnp.float32)
            * score_scale
        )
        return jnp.where(allowed, raw, MASKED)

    key_all, value_all = (
        lax.all_gather(keys, "blk", axis=1, tiled=True),
        lax.all_gather(values, "blk", axis=1, tiled=True),
    )
    scores = score_block(key_all)
    row_peak = jnp.max(scores, axis=-1, keepdims=True)
    expo = jnp.exp(scores - row_peak)
    row_total = jnp.sum(expo, axis=-1, keepdims=True)
    probs_b = (expo / row_total).astype(jnp.bfloat16)
    log_total = row_peak + jnp.log(row_total)
    attended = jnp.einsum(
        "rhqk,rkhd->rqhd",
        probs_b,
        value_all.reshape(rows_dev, -1, head_count, HD),
        preferred_element_type=jnp.float32,
    )
    attended_b = attended.reshape(tok_count, model_width).astype(jnp.bfloat16)
    middle = (
        embedded + jnp.dot(attended_b, out_weight, preferred_element_type=jnp.float32) + out_bias
    )
    normed_two = norm_apply(middle, norm2_gain, norm2_bias).astype(jnp.bfloat16)
    pre_act = jnp.dot(normed_two, fc1_weight, preferred_element_type=jnp.float32) + fc1_bias
    hidden_b = jax.nn.gelu(pre_act, approximate=False).astype(jnp.bfloat16)
    mlp_out = jnp.dot(hidden_b, fc2_weight, preferred_element_type=jnp.float32) + fc2_bias
    block_out = (
        (live_mask * (middle + mlp_out))
        .astype(jnp.bfloat16)
        .reshape(rows_dev, slice_len, model_width)
    )
    upstream = cotangent.reshape(tok_count, model_width).astype(jnp.float32) * live_mask
    upstream_b = upstream.astype(jnp.bfloat16)
    grad_fc2 = jnp.einsum("tf,td->fd", hidden_b, upstream_b, preferred_element_type=jnp.float32)
    grad_fc2_bias = jnp.sum(upstream_b.astype(jnp.float32), axis=0)
    hidden_grad = jnp.einsum(
        "td,fd->tf", upstream_b, fc2_weight, preferred_element_type=jnp.float32
    )
    gelu_out, gelu_pull = jax.vjp(partial(jax.nn.gelu, approximate=False), pre_act)
    pre_grad_b = gelu_pull(hidden_grad)[0].astype(jnp.bfloat16)
    grad_fc1 = jnp.einsum("td,tf->df", normed_two, pre_grad_b, preferred_element_type=jnp.float32)
    grad_fc1_bias = jnp.sum(pre_grad_b.astype(jnp.float32), axis=0)
    normed_two_grad = jnp.einsum(
        "tf,df->td", pre_grad_b, fc1_weight, preferred_element_type=jnp.float32
    )
    norm_out, norm_two_pull = jax.vjp(norm_apply, middle, norm2_gain, norm2_bias)
    middle_grad_norm, grad_gain_two, grad_bias_two = norm_two_pull(normed_two_grad)
    middle_grad = upstream + middle_grad_norm
    branch_grad_b = middle_grad.astype(jnp.bfloat16)
    grad_out = jnp.einsum(
        "td,te->de", attended_b, branch_grad_b, preferred_element_type=jnp.float32
    )
    grad_out_bias = jnp.sum(branch_grad_b.astype(jnp.float32), axis=0)
    attended_grad = jnp.einsum(
        "te,de->td", branch_grad_b, out_weight, preferred_element_type=jnp.float32
    )
    attended_grad = attended_grad.astype(jnp.bfloat16).reshape(rows_dev, slice_len, head_count, HD)
    key_heads_all = key_all.reshape(rows_dev, -1, head_count, HD)
    value_heads_all = value_all.reshape(rows_dev, -1, head_count, HD)
    probs = jnp.exp(score_block(key_all) - log_total)
    probs_back = probs.astype(jnp.bfloat16)
    prob_grad = jnp.einsum(
        "rqhd,rkhd->rhqk", attended_grad, value_heads_all, preferred_element_type=jnp.float32
    )
    score_grad_b = (
        probs * (prob_grad - jnp.sum(probs * prob_grad, axis=-1, keepdims=True))
    ).astype(jnp.bfloat16)
    query_grad = (
        jnp.einsum(
            "rhqk,rkhd->rqhd", score_grad_b, key_heads_all, preferred_element_type=jnp.float32
        )
        * score_scale
    )
    key_term = (
        jnp.einsum("rhqk,rqhd->krhd", score_grad_b, query, preferred_element_type=jnp.float32)
        * score_scale
    )
    value_term = jnp.einsum(
        "rhqk,rqhd->krhd", probs_back, attended_grad, preferred_element_type=jnp.float32
    )
    kv_grad = lax.psum_scatter(
        jnp.concatenate((key_term, value_term), axis=2)
        .reshape(lax.axis_size("blk") * slice_len, rows_dev, 2 * model_width)
        .astype(jnp.bfloat16),
        "blk",
        scatter_dimension=0,
        tiled=True,
    ).astype(jnp.float32)
    kv_grad = jnp.swapaxes(kv_grad, 0, 1).reshape(tok_count, 2 * model_width)
    packed_grad_b = jnp.concatenate(
        (query_grad.reshape(tok_count, model_width), kv_grad), axis=1
    ).astype(jnp.bfloat16)
    grad_qkv = jnp.einsum(
        "td,te->de", normed_one, packed_grad_b, preferred_element_type=jnp.float32
    )
    grad_query_bias = jnp.sum(packed_grad_b[:, :model_width].astype(jnp.float32), axis=0)
    grad_value_bias = jnp.sum(packed_grad_b[:, 2 * model_width :].astype(jnp.float32), axis=0)
    normed_one_grad = jnp.einsum(
        "te,de->td", packed_grad_b, qkv_weight, preferred_element_type=jnp.float32
    )
    norm_first, norm_one_pull = jax.vjp(norm_apply, embedded, norm1_gain, norm1_bias)
    stream_grad_norm, grad_gain_one, grad_bias_one = norm_one_pull(normed_one_grad)
    stream_grad_b = (middle_grad + stream_grad_norm).astype(jnp.bfloat16)
    pixel_grad = jnp.zeros((tok_count, pix_len), jnp.float32)
    emb_grads = []
    for band_index in range(band_count):
        band_col = band_hot[:, band_index : band_index + 1]
        masked_pixels = flat_pixels * band_col.astype(jnp.bfloat16)
        emb_grads.append(
            jnp.einsum(
                "tp,td->pd", masked_pixels, stream_grad_b, preferred_element_type=jnp.float32
            )
        )
        pixel_grad = pixel_grad + band_col * jnp.einsum(
            "td,pd->tp", stream_grad_b, emb_weight[band_index], preferred_element_type=jnp.float32
        )
    grad_emb = jnp.stack(emb_grads, axis=0)
    grad_emb_bias = jnp.einsum(
        "tg,td->gd", band_hot, stream_grad_b.astype(jnp.float32), precision=lax.Precision.HIGHEST
    )
    pixel_out = pixel_grad.astype(jnp.bfloat16).reshape(rows_dev, slice_len, pix_len)
    summed = (
        lax.psum_scatter(grad_emb, ("blk", "batch"), scatter_dimension=2, tiled=True),
        lax.psum_scatter(grad_emb_bias, ("blk", "batch"), scatter_dimension=1, tiled=True),
        lax.psum_scatter(grad_gain_one, ("blk", "batch"), scatter_dimension=0, tiled=True),
        lax.psum_scatter(grad_bias_one, ("blk", "batch"), scatter_dimension=0, tiled=True),
        lax.psum_scatter(grad_qkv, ("blk", "batch"), scatter_dimension=0, tiled=True),
        lax.psum_scatter(grad_query_bias, ("blk", "batch"), scatter_dimension=0, tiled=True),
        lax.psum_scatter(grad_value_bias, ("blk", "batch"), scatter_dimension=0, tiled=True),
        lax.psum_scatter(grad_out, ("blk", "batch"), scatter_dimension=0, tiled=True),
        lax.psum_scatter(grad_out_bias, ("blk", "batch"), scatter_dimension=0, tiled=True),
        lax.psum_scatter(grad_gain_two, ("blk", "batch"), scatter_dimension=0, tiled=True),
        lax.psum_scatter(grad_bias_two, ("blk", "batch"), scatter_dimension=0, tiled=True),
        lax.psum_scatter(grad_fc1, ("blk", "batch"), scatter_dimension=0, tiled=True),
        lax.psum_scatter(grad_fc1_bias, ("blk", "batch"), scatter_dimension=0, tiled=True),
        lax.psum_scatter(grad_fc2, ("blk", "batch"), scatter_dimension=0, tiled=True),
        lax.psum_scatter(grad_fc2_bias, ("blk", "batch"), scatter_dimension=0, tiled=True),
    )
    return (
        block_out,
        pixel_out,
        summed[0],
        summed[1],
        summed[2],
        summed[3],
        summed[4],
        summed[5],
        summed[6],
        summed[7],
        summed[8],
        summed[9],
        summed[10],
        summed[11],
        summed[12],
        summed[13],
        summed[14],
    )


def solution(mesh):
    return jax.shard_map(
        on_device,
        mesh=mesh,
        in_specs=(
            P("batch", "blk", None),
            P("batch", "blk", None),
            P("batch", None),
            P("batch", "blk"),
            P("batch", "blk", None),
            P(),
            P(),
            P(),
            P(),
            P(),
            P(),
            P(),
            P(),
            P(),
            P(),
            P(),
            P(),
            P(),
            P(),
            P(),
        ),
        out_specs=(
            P("batch", "blk", None),
            P("batch", "blk", None),
            P(None, None, ("blk", "batch")),
            P(None, ("blk", "batch")),
            P(("blk", "batch")),
            P(("blk", "batch")),
            P(("blk", "batch"), None),
            P(("blk", "batch")),
            P(("blk", "batch")),
            P(("blk", "batch"), None),
            P(("blk", "batch")),
            P(("blk", "batch")),
            P(("blk", "batch")),
            P(("blk", "batch"), None),
            P(("blk", "batch")),
            P(("blk", "batch"), None),
            P(("blk", "batch")),
        ),
        check_vma=False,
    )
```

profile of v0, /device:TPU:0, one launch (start us, length us, event | category | flops | bytes accessed | tf_op | source)
XLA Modules:
  0.0 3204.0 jit_solution(13715723716560471983)
XLA Ops:
  8.7 2.2 fusion.54
  10.9 2.1 fusion.57
  13.1 2.1 fusion.60
  16.0 2.4 fusion.133
  19.3 1.9 fusion.126
  23.9 2.8 fusion.97
  27.2 2.0 copy.52
  30.7 22.3 all-gather.7.cloned.1.call-done
  53.0 3.9 copy.53
  56.9 5.0 fusion.134
  62.0 3.8 fusion
  65.8 2.4 copy-done.2
  68.8 12.0 all-gather.5.cloned.1.call-done
  80.8 4.0 copy.51
  84.7 8.3 fusion.89
  94.3 15.5 multiply_convert_fusion.2
  109.8 11.7 convert_reduce_fusion
  121.5 7.4 multiply_reduce_fusion.1
  134.9 14.5 multiply_reduce_fusion
  149.4 9.4 convert_bitcast_fusion
  158.8 8.0 multiply_convert_fusion
  166.8 3.3 copy-done.3
  171.6 2.4 pad_maximum_fusion.1
  175.6 6.1 fusion.67
  183.3 41.7 %reduce-scatter.7.cloned.1.call-done = bf16[256,1,2048]{0,2,1:T(8,128)(2,1)} async-done(((bf16[1024,1,2048]{0,2,1:T(8,128)(2,1)}), bf16[256,1,2048]{0,2,1:T(8,128)(2,1)}) %reduce-scatter.7.cloned.1.call-update) | async-done | bytes 1048592 | tf_op jit(solution)/shard_map/reduce_scatter | solution.py:171
  225.0 1.8 convert_reduce_fusion.3
  226.9 6.1 multiply_reduce_fusion.2
  234.6 2.3 convolution_bitcast_fusion
  236.9 2.4 convolution_bitcast_fusion.1
  239.2 2.4 convolution_bitcast_fusion.2
  241.7 2.4 convolution_bitcast_fusion.3
  244.1 10.6 pad_maximum_fusion
  254.7 14.8 copy.55
  270.8 2.7 fusion.136
  274.7 9.9 fusion.127
  285.3 7.9 fusion.101
  293.2 9.8 fusion.120
  303.7 7.2 fusion.93
  310.9 2.0 fusion.80
  313.0 2.3 fusion.83
  315.3 2.2 fusion.86
  317.5 2.8 fusion.94
  320.4 64.4 %all-reduce.17.cloned.1.call-done = (f32[4,1024]{1,0:T(4,128)}, f32[1024]{0:T(1024)}, f32[1024]{0:T(1024)}, f32[1024]{0:T(1024)}, f32[1024]{0:T(1024)}, /*index=...) async-done(((f32[4,1024]{1,0:T(4,128)}, f32[1024]{0:T(1024)}, f32[1024]{0:T(1024)}, f32[1024]{0:T(1024)}, f32[1024]{0:T(1024)}, ...) | async-done | bytes 65552
  397.3 160.9 %all-reduce.15.cloned.1.call-done = f32[4,768,1024]{1,0,2:T(4,128)} async-done(((f32[4,768,1024]{1,0,2:T(4,128)}), f32[4,768,1024]{1,0,2:T(4,128)}) %all-reduce.15.cloned.1.call-update) | async-done | bytes 12582928
  559.8 644.3 %reduce-scatter.11.cloned.1.call-done = f32[8,1024]{1,0:T(8,128)} async-done(((f32[1024,1024]{1,0:T(8,128)}), f32[8,1024]{1,0:T(8,128)}) %reduce-scatter.11.cloned.1.call-update) | async-done | bytes 32784 | tf_op jit(solution)/shard_map/reduce_scatter | solution.py:220
  1204.1 667.8 %reduce-scatter.13.cloned.1.call-done = f32[8,4096]{1,0:T(8,128)} async-done(((f32[1024,4096]{1,0:T(8,128)}), f32[8,4096]{1,0:T(8,128)}) %reduce-scatter.13.cloned.1.call-update) | async-done | bytes 131088 | tf_op jit(solution)/shard_map/reduce_scatter | solution.py:224
  1871.9 657.7 %reduce-scatter.9.cloned.1.call-done = f32[8,3072]{1,0:T(8,128)} async-done(((f32[1024,3072]{1,0:T(8,128)}), f32[8,3072]{1,0:T(8,128)}) %reduce-scatter.9.cloned.1.call-update) | async-done | bytes 98320 | tf_op jit(solution)/shard_map/reduce_scatter | solution.py:217
  2529.7 667.3 %reduce-scatter.15.cloned.1.call-done = f32[32,1024]{1,0:T(8,128)} async-done(((f32[4096,1024]{1,0:T(8,128)}), f32[32,1024]{1,0:T(8,128)}) %reduce-scatter.15.cloned.1.call-update) | async-done | bytes 131088 | tf_op jit(solution)/shard_map/reduce_scatter | solution.py:226
  (212 shorter events, 39.7 us)
Async XLA Ops:
  7.2 85.9 %copy-start = (bf16[1024,1024]{1,0:T(8,128)(2,1)S(1)}, bf16[1024,1024]{1,0:T(8,128)(2,1)}, u32[]{:S(2)}) copy-start(bf16[1024,1024]{1,0:T(8,128)(2,1)} %param.32) | copy-start | bytes 6291460
  7.2 5.8 copy-start.9
  7.2 45.8 %all-gather.7.cloned.1.call-start = ((), (), s32[]{:S(2)}) async-start(), calls=%async_computation.11 | async-start | bytes 2621440 | tf_op jit(solution)/shard_map/all_gather | solution.py:94
  8.1 4.9 copy-start.65
  8.2 4.9 copy-start.67
  8.2 7.0 copy-start.63
  8.2 7.8 copy-start.54
  8.7 6.5 copy-start.23
  8.7 6.5 copy-start.44
  8.7 6.5 copy-start.50
  13.1 6.2 slice-start.4
  22.9 6.3 copy-start.56
  23.8 57.0 %all-gather.5.cloned.1.call-start = ((), (), s32[]{:S(2)}) async-start(), calls=%async_computation.10 | async-start | bytes 2621440 | tf_op jit(solution)/shard_map/all_gather | solution.py:95
  26.6 198.3 %reduce-scatter.7.cloned.1.call-start = ((), (), s32[]{:S(2)}) async-start(), calls=%async_computation.5 | async-start | bytes 5242880 | tf_op jit(solution)/shard_map/reduce_scatter | solution.py:171
  62.0 6.2 copy-start.2
  62.0 6.2 copy-start.28
  84.7 8.3 copy-start.47
  93.0 16.7 copy-start.17
  93.9 35.0 %copy-start.7 = (f32[256,1024]{1,0:T(8,128)}, f32[256,1024]{1,0:T(8,128)S(1)}, u32[]{:S(2)}) copy-start(f32[256,1024]{1,0:T(8,128)S(1)} %get-tuple-element.110) | copy-start | bytes 3145732
  93.9 35.0 %copy-start.36 = (f32[256]{0:T(256)}, f32[256]{0:T(256)S(1)}, u32[]{:S(2)}) copy-start(f32[256]{0:T(256)S(1)} %broadcast_multiply_fusion) | copy-start | bytes 3076
  94.2 34.7 %copy-start.40 = (f32[256]{0:T(256)}, f32[256]{0:T(256)S(1)}, u32[]{:S(2)}) copy-start(f32[256]{0:T(256)S(1)} %fusion.117) | copy-start | bytes 3076
  94.2 15.5 copy-start.14
  94.2 15.5 copy-start.42
  121.5 7.4 copy-start.22
  134.8 23.9 slice-start
  134.9 23.9 slice-start.1
  134.9 23.9 slice-start.2
  149.4 9.4 slice-start.3
  158.8 11.3 copy-start.13
  174.0 210.7 %all-reduce.17.cloned.1.call-start = ((), (), s32[]{:S(2)}) async-start(), calls=%async_computation.13 | async-start | bytes 131072
  175.6 51.3 %copy-start.30 = (f32[1024]{0:T(1024)S(1)}, f32[1024]{0:T(1024)}, u32[]{:S(2)}) copy-start(f32[1024]{0:T(1024)} %param.27) | copy-start | bytes 12292
  175.6 51.3 %copy-start.39 = (f32[256]{0:T(256)S(1)}, f32[256]{0:T(256)}, u32[]{:S(2)}) copy-start(f32[256]{0:T(256)} %copy-done.38) | copy-start | bytes 3076
  175.6 51.3 %copy-start.46 = (f32[256]{0:T(256)S(1)}, f32[256]{0:T(256)}, u32[]{:S(2)}) copy-start(f32[256]{0:T(256)} %copy-done.45) | copy-start | bytes 3076
  226.8 6.1 copy-start.53
  226.8 6.6 copy-start.11
  226.9 6.6 copy-start.15
  226.9 6.6 copy-start.43
  226.9 6.5 copy-start.49
  233.8 77.1 %copy-start.4 = (bf16[256,1024]{1,0:T(8,128)(2,1)}, bf16[256,1024]{1,0:T(8,128)(2,1)S(1)}, u32[]{:S(2)}) copy-start(bf16[256,1024]{1,0:T(8,128)(2,1)S(1)} %add_convert_fusion.1) | copy-start | bytes 1572868
  236.9 4.8 copy-start.59
  244.1 314.2 %all-reduce.15.cloned.1.call-start = ((), (), s32[]{:S(2)}) async-start(), calls=%async_computation.12 | async-start | bytes 25165824
  269.6 934.5 %reduce-scatter.11.cloned.1.call-start = ((), (), s32[]{:S(2)}) async-start(), calls=%async_computation.7 | async-start | bytes 4227072 | tf_op jit(solution)/shard_map/reduce_scatter | solution.py:220
  273.5 1598.4 %reduce-scatter.13.cloned.1.call-start = ((), (), s32[]{:S(2)}) async-start(), calls=%async_computation.8 | async-start | bytes 16908288 | tf_op jit(solution)/shard_map/reduce_scatter | solution.py:224
  284.6 2245.1 %reduce-scatter.9.cloned.1.call-start = ((), (), s32[]{:S(2)}) async-start(), calls=%async_computation.6 | async-start | bytes 12681216 | tf_op jit(solution)/shard_map/reduce_scatter | solution.py:217
  293.2 2903.9 %reduce-scatter.15.cloned.1.call-start = ((), (), s32[]{:S(2)}) async-start(), calls=%async_computation.9 | async-start | bytes 16908288 | tf_op jit(solution)/shard_map/reduce_scatter | solution.py:226
  303.7 7.2 copy-start.68
  303.7 9.2 copy-start.66
  313.0 2884.1 %copy-start.1 = (bf16[1024,1024]{1,0:T(8,128)(2,1)S(1)}, bf16[1024,1024]{1,0:T(8,128)(2,1)}, u32[]{:S(2)}) copy-start(bf16[1024,1024]{1,0:T(8,128)(2,1)} %param.32) | copy-start | bytes 6291460
  (38 other events, 76.4 us)
Sparse Core Ops, SparseCore 0:
  23.9 29.0 all-gather.6
  54.7 26.0 all-gather.4
  174.1 50.8 reduce-scatter.6
  244.2 140.4 all-reduce.16
  389.5 168.7 all-reduce.14
  561.2 642.8 reduce-scatter.10
  1207.1 664.8 reduce-scatter.12
  1874.9 654.7 reduce-scatter.8
  2532.8 664.2 reduce-scatter.14
where the time goes:
time: 3210 us; the launch traced here: 3200 us
  waiting for transfers between devices  2940 us (92%)
  matrix products  156 us (5%)
  local copies, waits for them, and re-layouts  57.8 us (2%)
  other arithmetic  35.1 us (1%)
    reduce_scatter x1, waiting for transfers between devices, on_device(): lax.psum_scatter(grad_fc1, ('blk', 'batch'), scatter_dimension=0, tiled=T...  668 us
    reduce_scatter x1, waiting for transfers between devices, on_device(): lax.psum_scatter(grad_fc2, ('blk', 'batch'), scatter_dimension=0, tiled=T...  667 us
    reduce_scatter x1, waiting for transfers between devices, on_device(): lax.psum_scatter(grad_qkv, ('blk', 'batch'), scatter_dimension=0, tiled=T...  658 us
    reduce_scatter x1, waiting for transfers between devices, on_device(): lax.psum_scatter(grad_out, ('blk', 'batch'), scatter_dimension=0, tiled=T...  644 us
    unnamed x11, waiting for transfers between devices  225 us
  transfers between devices with their start and end apart: 9, of which 9 were waited for; matrix products, arithmetic and copies ran while one was open for 4% of the time, Pallas kernels for 0%

commit v1 on v0

--- a/solution.py
+++ b/solution.py
@@ -3,6 +3,8 @@
 import jax
 import jax.numpy as jnp
 from jax import lax
+from jax.experimental import pallas as pl
+from jax.experimental.pallas import tpu as pltpu
 from jax.sharding import PartitionSpec as P
 
 HD = 64
@@ -10,6 +12,345 @@
 
 NORM_EPS = 1e-06
 MASKED = -1e30
+
+
+MESH = pl.DeviceIdType.MESH
+AXES = ("xb", "xa", "yb", "ya", "zb", "za")
+ROTATION = ("xa", "ya", "za", "xb", "yb", "zb")
+GRAY = (0, 1, 3, 2)
+BLOCKS = tuple(16 * x + 4 * y + z for x in GRAY for y in GRAY for z in GRAY)
+CHUNKS = 30
+
+
+def place():
+    blk = lax.axis_index("blk")
+    batch = lax.axis_index("batch")
+    return blk // 2, blk % 2, batch // 16, (batch // 4) % 4, batch % 4
+
+
+def neighbours(where):
+    x_hi, core, x_lo, y, z = where
+
+    def device(x_hi, core, x_lo, y, z):
+        return (x_hi * 2 + core, x_lo * 16 + y * 4 + z)
+
+    return {
+        "core": device(x_hi, 1 - core, x_lo, y, z),
+        "xa": device(x_hi, core, 1 - x_lo, y, z),
+        "xb": device(1 - x_hi, core, 1 - x_lo, y, z),
+        "ya": device(x_hi, core, x_lo, y + 1 - 2 * (y % 2), z),
+        "yb": device(x_hi, core, x_lo, 3 - y, z),
+        "za": device(x_hi, core, x_lo, y, z + 1 - 2 * (z % 2)),
+        "zb": device(x_hi, core, x_lo, y, 3 - z),
+    }
+
+
+def own_bits(where):
+    x_hi, _, x_lo, y, z = where
+    return {
+        "xb": x_hi,
+        "xa": (x_hi + x_lo) % 2,
+        "yb": y // 2,
+        "ya": (y // 2 + y) % 2,
+        "zb": z // 2,
+        "za": (z // 2 + z) % 2,
+    }
+
+
+def class_dims(kind):
+    return tuple(ROTATION[(kind + step) % 6] for step in range(6))
+
+
+def split_shape(kind, step):
+    dims = class_dims(kind)
+    left = [axis for axis in AXES if axis not in dims[:step]]
+    at = left.index(dims[step])
+    return 2**at, 2 ** (len(left) - 1 - at)
+
+
+KEEP_AT = (0, 32, 0, 16, 24, 28)
+SEND_AT = (32, 48, 8, 20, 26, 29)
+ARRIVE_AT = (0, 32, 48, 56, 60, 62)
+
+
+def weight_grads_kernel(
+    gs_in, pix_in, hot_in, n1_in, gp_in, att_in, gb_in, n2_in, gpre_in, hid_in, gout_in, row_in,
+    emb_out, qkv_out, out_out, fc1_out, fc2_out, bias_out,
+    x_buf, xh_buf, pix_buf, hot_buf, gp_buf, gb_buf, gpre_buf, gout_buf, row_buf, lanes,
+    xt_buf, xht_buf, work, arrive, work_f, arrive_f,
+    ex_send, ex_recv, ex_local, send_sem, recv_sem,
+):
+    where = place()
+    x_hi, core, x_lo, y, z = where
+    near = neighbours(where)
+    bits = own_bits(where)
+
+    barrier = pltpu.get_barrier_semaphore()
+    for target in near.values():
+        pl.semaphore_signal(barrier, inc=1, device_id=target, device_id_type=MESH)
+    pl.semaphore_wait(barrier, 7)
+
+    count = 0
+
+    def exchange(source, dest, width):
+        nonlocal count
+        index, count = count, count + 1
+
+        def cut(owner):
+            if width is None:
+                return source
+            return source.at[:, pl.ds(pl.multiple_of(width[0] + owner * width[1], 128), width[1])]
+
+        local = pltpu.make_async_copy(cut(core), dest(0), ex_local.at[index])
+        remote = pltpu.make_async_remote_copy(
+            src_ref=cut(1 - core),
+            dst_ref=dest(1),
+            send_sem=ex_send.at[index],
+            recv_sem=ex_recv.at[index],
+            device_id=near["core"],
+            device_id_type=MESH,
+        )
+        return local, remote
+
+    def slots(buf, columns=None):
+        def dest(half):
+            if columns is None:
+                return buf.at[pl.ds(256 * half, 256), :]
+            return buf.at[pl.ds(256 * half, 256), pl.ds(*columns)]
+
+        return dest
+
+    def halves(source, buf, span):
+        return [
+            exchange(source, slots(buf, (high * span, span)), (high * 2 * span, span))
+            for high in (0, 1)
+        ]
+
+    groups = {
+        "rows": [exchange(row_in, lambda half: row_buf.at[half], None)],
+        "out": halves(att_in, x_buf.at[0], 256) + [exchange(gb_in, slots(gb_buf), None)],
+        "qkv": halves(n1_in, x_buf.at[1], 256) + [exchange(gp_in, slots(gp_buf), None)],
+        "fc1": halves(n2_in, x_buf.at[2], 256) + [exchange(gpre_in, slots(gpre_buf), None)],
+        "emb": halves(gs_in, x_buf.at[3], 256)
+        + [exchange(pix_in, slots(pix_buf), None), exchange(hot_in, slots(hot_buf), None)],
+        "fc2": halves(hid_in, xh_buf, 1024) + [exchange(gout_in, slots(gout_buf), None)],
+    }
+
+    def begin(name):
+        for local, remote in groups[name]:
+            remote.start()
+            local.start()
+
+    def arrived(name):
+        for local, remote in groups[name]:
+            local.wait()
+            remote.wait_recv()
+
+    def transposed(buf, dest):
+        turned = buf[...].astype(jnp.float32).T
+        dest[...] = jnp.concatenate(
+            [turned[8 * block : 8 * block + 8] for block in BLOCKS], axis=0
+        ).astype(jnp.bfloat16)
+
+    def hop(chunk, kind, step, floats=False):
+        held, come, index = (
+            (work_f, arrive_f, CHUNKS) if floats else (work.at[chunk], arrive.at[chunk], chunk)
+        )
+        half = 32 >> step
+        return pltpu.make_async_remote_copy(
+            src_ref=held.at[pl.ds(SEND_AT[step], half)],
+            dst_ref=come.at[pl.ds(ARRIVE_AT[step], half)],
+            send_sem=send_sem.at[index, step],
+            recv_sem=recv_sem.at[index, step],
+            device_id=near[class_dims(kind)[step]],
+            device_id_type=MESH,
+        )
+
+    def put(chunk, kind, result, floats=False):
+        held = work_f if floats else work.at[chunk]
+        before, after = split_shape(kind, 0)
+        own = bits[class_dims(kind)[0]]
+        for a in range(before):
+            for bit in (0, 1):
+                other = own if bit == 0 else 1 - own
+                piece = result[(2 * a + bit) * after : (2 * a + bit + 1) * after]
+                held[pl.ds(other * 32 + a * after, after)] = piece
+        hop(chunk, kind, 0, floats).start()
+
+    def advance(chunk, kind, step, finish, floats=False):
+        held, come = (work_f, arrive_f) if floats else (work.at[chunk], arrive.at[chunk])
+        hop(chunk, kind, step, floats).wait_recv()
+        keep, come_at = KEEP_AT[step], ARRIVE_AT[step]
+        if step == 5:
+            finish(held[keep].astype(jnp.float32) + come[come_at].astype(jnp.float32))
+            return
+        if step == 0:
+            hop(chunk, kind, 0, floats).wait_send()
+        before, after = split_shape(kind, step + 1)
+        own = bits[class_dims(kind)[step + 1]]
+        for bit, base in ((1 - own, SEND_AT[step + 1]), (own, KEEP_AT[step + 1])):
+
+            def merge(a, carry, bit=bit, base=base):
+                at = (2 * a + bit) * after
+                held[pl.ds(base + a * after, after)] = (
+                    held[pl.ds(keep + at, after)] + come[pl.ds(come_at + at, after)]
+                )
+                return carry
+
+            lax.fori_loop(0, before, merge, 0, unroll=min(before, 8))
+            if base == SEND_AT[step + 1]:
+                hop(chunk, kind, step + 1, floats).start()
+
+    def pair(left, right, tile):
+        a = jnp.dot(left, right(2 * tile), preferred_element_type=jnp.float32)
+        b = jnp.dot(left, right(2 * tile + 1), preferred_element_type=jnp.float32)
+        return jnp.concatenate(
+            (a.reshape(64, 8, 256), b.reshape(64, 8, 256)), axis=1
+        ).astype(jnp.bfloat16)
+
+    def columns_of(buf):
+        return lambda tile: buf[:, 256 * tile : 256 * tile + 256]
+
+    def band_pixels(tile):
+        band, at = tile // 3, tile % 3
+        picked = pix_buf[:, 256 * at : 256 * at + 256].astype(jnp.float32)
+        chosen = hot_buf[:, band : band + 1].astype(jnp.float32)
+        return (picked * chosen).astype(jnp.bfloat16)
+
+    plan = []
+    for name, x_at, right, tiles, dest in (
+        ("out", 0, columns_of(gb_buf), 2, out_out),
+        ("qkv", 1, columns_of(gp_buf), 6, qkv_out),
+        ("fc1", 2, columns_of(gpre_buf), 8, fc1_out),
+        ("emb", 3, band_pixels, 6, emb_out),
+    ):
+        for tile in range(tiles):
+            plan.append((name, x_at, right, tile, dest))
+    for tile in range(8):
+        plan.append(("fc2", None, columns_of(gout_buf), tile, fc2_out))
+
+    def finisher(chunk):
+        name, _, _, tile, dest = plan[chunk]
+
+        def finish(total):
+            if name == "fc2":
+                dest[
+                    16 * (tile % 2) : 16 * (tile % 2) + 16, 256 * (tile // 2) : 256 * (tile // 2) + 256
+                ] = total
+            else:
+                dest[:, 512 * tile : 512 * tile + 256] = total[:8]
+                dest[:, 512 * tile + 256 : 512 * tile + 512] = total[8:]
+
+        return finish
+
+    def finish_bias(total):
+        bias_out[...] = total
+
+    ready = set()
+
+    def compute(chunk):
+        name, x_at, right, tile, _ = plan[chunk]
+        if name not in ready:
+            ready.add(name)
+            arrived(name)
+            if name == "fc2":
+                turned = xh_buf[...].astype(jnp.float32).T.astype(jnp.bfloat16)
+                xht_buf[...] = jnp.concatenate(
+                    [turned[32 * block : 32 * block + 32] for block in BLOCKS], axis=0
+                )
+            else:
+                transposed(x_buf.at[x_at], xt_buf.at[x_at])
+        if name != "fc2":
+            put(chunk, chunk % 6, pair(xt_buf[x_at], right, tile))
+        elif tile % 2 == 0:
+            both = jnp.dot(
+                xht_buf[...], right(tile // 2), preferred_element_type=jnp.float32
+            ).reshape(64, 32, 256)
+            put(chunk, chunk % 6, both[:, :16].astype(jnp.bfloat16))
+            put(chunk + 1, (chunk + 1) % 6, both[:, 16:].astype(jnp.bfloat16))
+
+    begin("rows")
+    begin("out")
+    begin("qkv")
+    waves = CHUNKS // 6
+    for turn in range(waves + 6):
+        if turn < waves:
+            for chunk in range(6 * turn, 6 * turn + 6):
+                compute(chunk)
+            if turn == 0:
+                begin("fc1")
+                begin("emb")
+                arrived("rows")
+                lanes[...] = jnp.zeros_like(lanes)
+                for high in (0, 1):
+                    span = pl.ds(pl.multiple_of(high * 512 + core * 256, 128), 256)
+                    lanes[0:16, 256 * high : 256 * high + 256] = (
+                        row_buf[0, :, span] + row_buf[1, :, span]
+                    )
+                turned = lanes[...].T.reshape(64, 8, 128)
+                put(None, 0, jnp.concatenate([turned[b : b + 1] for b in BLOCKS], axis=0), True)
+            if turn == 1:
+                begin("fc2")
+        for step in range(6):
+            wave = turn - 1 - step
+            if 0 <= wave < waves:
+                for chunk in range(6 * wave, 6 * wave + 6):
+                    advance(chunk, chunk % 6, step, finisher(chunk))
+                if wave == 0:
+                    advance(None, 0, step, finish_bias, True)
+    for name in groups:
+        for _, remote in groups[name]:
+            remote.wait_send()
+    for step in range(1, 6):
+        for chunk in range(CHUNKS):
+            hop(chunk, chunk % 6, step).wait_send()
+        hop(None, 0, step, True).wait_send()
+
+
+def weight_grads(*operands):
+    any_space = pl.BlockSpec(memory_space=pl.ANY)
+    in_vmem = pl.BlockSpec(memory_space=pltpu.VMEM)
+    half, full = jnp.bfloat16, jnp.float32
+    return pl.pallas_call(
+        weight_grads_kernel,
+        out_shape=(
+            jax.ShapeDtypeStruct((8, 3072), full),
+            jax.ShapeDtypeStruct((8, 3072), full),
+            jax.ShapeDtypeStruct((8, 1024), full),
+            jax.ShapeDtypeStruct((8, 4096), full),
+            jax.ShapeDtypeStruct((32, 1024), full),
+            jax.ShapeDtypeStruct((8, 128), full),
+        ),
+        in_specs=[any_space] * 12,
+        out_specs=(in_vmem,) * 6,
+        scratch_shapes=[
+            pltpu.VMEM((4, 512, 512), half),
+            pltpu.VMEM((512, 2048), half),
+            pltpu.VMEM((512, 768), half),
+            pltpu.VMEM((512, 128), half),
+            pltpu.VMEM((512, 3072), half),
+            pltpu.VMEM((512, 1024), half),
+            pltpu.VMEM((512, 4096), half),
+            pltpu.VMEM((512, 1024), half),
+            pltpu.VMEM((2, 16, 1024), full),
+            pltpu.VMEM((128, 512), full),
+            pltpu.VMEM((4, 512, 512), half),
+            pltpu.VMEM((2048, 512), half),
+            pltpu.VMEM((CHUNKS, 64, 16, 256), half),
+            pltpu.VMEM((CHUNKS, 63, 16, 256), half),
+            pltpu.VMEM((64, 8, 128), full),
+            pltpu.VMEM((63, 8, 128), full),
+            pltpu.SemaphoreType.DMA((20,)),
+            pltpu.SemaphoreType.DMA((20,)),
+            pltpu.SemaphoreType.DMA((20,)),
+            pltpu.SemaphoreType.DMA((CHUNKS + 1, 6)),
+            pltpu.SemaphoreType.DMA((CHUNKS + 1, 6)),
+        ],
+        compiler_params=pltpu.CompilerParams(
+            collective_id=0, has_side_effects=True, vmem_limit_bytes=60 << 20
+        ),
+        name="weight_grads",
+    )(*operands)
 
 
 def normalize(values):
@@ -121,14 +462,12 @@
     )
     upstream = cotangent.reshape(tok_count, model_width).astype(jnp.float32) * live_mask
     upstream_b = upstream.astype(jnp.bfloat16)
-    grad_fc2 = jnp.einsum("tf,td->fd", hidden_b, upstream_b, preferred_element_type=jnp.float32)
     grad_fc2_bias = jnp.sum(upstream_b.astype(jnp.float32), axis=0)
     hidden_grad = jnp.einsum(
         "td,fd->tf", upstream_b, fc2_weight, preferred_element_type=jnp.float32
     )
     gelu_out, gelu_pull = jax.vjp(partial(jax.nn.gelu, approximate=False), pre_act)
     pre_grad_b = gelu_pull(hidden_grad)[0].astype(jnp.bfloat16)
-    grad_fc1 = jnp.einsum("td,tf->df", normed_two, pre_grad_b, preferred_element_type=jnp.float32)
     grad_fc1_bias = jnp.sum(pre_grad_b.astype(jnp.float32), axis=0)
     normed_two_grad = jnp.einsum(
         "tf,df->td", pre_grad_b, fc1_weight, preferred_element_type=jnp.float32
@@ -137,9 +476,6 @@
     middle_grad_norm, grad_gain_two, grad_bias_two = norm_two_pull(normed_two_grad)
     middle_grad = upstream + middle_grad_norm
     branch_grad_b = middle_grad.astype(jnp.bfloat16)
-    grad_out = jnp.einsum(
-        "td,te->de", attended_b, branch_grad_b, preferred_element_type=jnp.float32
-    )
     grad_out_bias = jnp.sum(branch_grad_b.astype(jnp.float32), axis=0)
     attended_grad = jnp.einsum(
         "te,de->td", branch_grad_b, out_weight, preferred_element_type=jnp.float32
@@ -180,9 +516,6 @@
     packed_grad_b = jnp.concatenate(
         (query_grad.reshape(tok_count, model_width), kv_grad), axis=1
     ).astype(jnp.bfloat16)
-    grad_qkv = jnp.einsum(
-        "td,te->de", normed_one, packed_grad_b, preferred_element_type=jnp.float32
-    )
     grad_query_bias = jnp.sum(packed_grad_b[:, :model_width].astype(jnp.float32), axis=0)
     grad_value_bias = jnp.sum(packed_grad_b[:, 2 * model_width :].astype(jnp.float32), axis=0)
     normed_one_grad = jnp.einsum(
@@ -192,39 +525,65 @@
     stream_grad_norm, grad_gain_one, grad_bias_one = norm_one_pull(normed_one_grad)
     stream_grad_b = (middle_grad + stream_grad_norm).astype(jnp.bfloat16)
     pixel_grad = jnp.zeros((tok_count, pix_len), jnp.float32)
-    emb_grads = []
     for band_index in range(band_count):
         band_col = band_hot[:, band_index : band_index + 1]
-        masked_pixels = flat_pixels * band_col.astype(jnp.bfloat16)
-        emb_grads.append(
-            jnp.einsum(
-                "tp,td->pd", masked_pixels, stream_grad_b, preferred_element_type=jnp.float32
-            )
-        )
         pixel_grad = pixel_grad + band_col * jnp.einsum(
             "td,pd->tp", stream_grad_b, emb_weight[band_index], preferred_element_type=jnp.float32
         )
-    grad_emb = jnp.stack(emb_grads, axis=0)
     grad_emb_bias = jnp.einsum(
         "tg,td->gd", band_hot, stream_grad_b.astype(jnp.float32), precision=lax.Precision.HIGHEST
     )
     pixel_out = pixel_grad.astype(jnp.bfloat16).reshape(rows_dev, slice_len, pix_len)
+    bias_rows = jnp.concatenate(
+        (
+            grad_emb_bias,
+            jnp.stack(
+                (
+                    grad_gain_one,
+                    grad_bias_one,
+                    grad_query_bias,
+                    grad_value_bias,
+                    grad_out_bias,
+                    grad_gain_two,
+                    grad_bias_two,
+                    grad_fc2_bias,
+                )
+            ),
+            jnp.swapaxes(grad_fc1_bias.reshape(128, 4, 8), 0, 1).reshape(4, 1024),
+        )
+    )
+    hot_lanes = jnp.pad(band_hot, ((0, 0), (0, 128 - band_count))).astype(jnp.bfloat16)
+    emb_sum, qkv_sum, out_sum, fc1_sum, fc2_sum, bias_sum = weight_grads(
+        stream_grad_b,
+        flat_pixels,
+        hot_lanes,
+        normed_one,
+        packed_grad_b,
+        attended_b,
+        branch_grad_b,
+        normed_two,
+        pre_grad_b,
+        hidden_b,
+        upstream_b,
+        bias_rows,
+    )
+    bias_cols = bias_sum[:, :16].T
     summed = (
-        lax.psum_scatter(grad_emb, ("blk", "batch"), scatter_dimension=2, tiled=True),
-        lax.psum_scatter(grad_emb_bias, ("blk", "batch"), scatter_dimension=1, tiled=True),
-        lax.psum_scatter(grad_gain_one, ("blk", "batch"), scatter_dimension=0, tiled=True),
-        lax.psum_scatter(grad_bias_one, ("blk", "batch"), scatter_dimension=0, tiled=True),
-        lax.psum_scatter(grad_qkv, ("blk", "batch"), scatter_dimension=0, tiled=True),
-        lax.psum_scatter(grad_query_bias, ("blk", "batch"), scatter_dimension=0, tiled=True),
-        lax.psum_scatter(grad_value_bias, ("blk", "batch"), scatter_dimension=0, tiled=True),
-        lax.psum_scatter(grad_out, ("blk", "batch"), scatter_dimension=0, tiled=True),
-        lax.psum_scatter(grad_out_bias, ("blk", "batch"), scatter_dimension=0, tiled=True),
-        lax.psum_scatter(grad_gain_two, ("blk", "batch"), scatter_dimension=0, tiled=True),
-        lax.psum_scatter(grad_bias_two, ("blk", "batch"), scatter_dimension=0, tiled=True),
-        lax.psum_scatter(grad_fc1, ("blk", "batch"), scatter_dimension=0, tiled=True),
-        lax.psum_scatter(grad_fc1_bias, ("blk", "batch"), scatter_dimension=0, tiled=True),
-        lax.psum_scatter(grad_fc2, ("blk", "batch"), scatter_dimension=0, tiled=True),
-        lax.psum_scatter(grad_fc2_bias, ("blk", "batch"), scatter_dimension=0, tiled=True),
+        emb_sum.T.reshape(band_count, pix_len, 8),
+        bias_cols[0:4],
+        bias_cols[4],
+        bias_cols[5],
+        qkv_sum,
+        bias_cols[6],
+        bias_cols[7],
+        out_sum,
+        bias_cols[8],
+        bias_cols[9],
+        bias_cols[10],
+        fc1_sum,
+        bias_cols[12:16].reshape(32),
+        fc2_sum,
+        bias_cols[11],
     )
     return (
         block_out,

time: 3210 us -> 341 us (0.11)
  waiting for transfers between devices: 2940 us -> 56.8 us
  Pallas kernels: 0 us -> 81.6 us
  matrix products: 156 us -> 102 us
    reduce_scatter x4 -> x0, waiting for transfers between devices: 2640 us -> none  [the longest x1 668 us: on_device(): lax.psum_scatter(grad_fc1, ('blk', 'batch'), scatter_dimension=0, tiled=T...]
    unnamed x11 -> x3, waiting for transfers between devices: 225 us -> 0.05 us
    pallas_call x0 -> x1, Pallas kernels: none -> 81.6 us  [weight_grads(): pl.pallas_call(weight_grads_kernel, out_shape=(jax.ShapeDtypeStruct((8, 3...]
    dot_general x8 -> x0, matrix products: 39.7 us -> none  [the longest x1 9.86 us: on_device(): jnp.einsum('td,tf->df', normed_two, pre_grad_b, preferred_element_type=jn...]
  transfers between devices with their start and end apart: 9 -> 3, of which waited for: 9 -> 3; matrix products, arithmetic and copies ran while one was open for 4% -> 14% of each run, Pallas kernels for 0% -> 0%
where the time goes in v1:
time: 341 us; the launch traced here: 336 us
  matrix products  102 us (30%)
  Pallas kernels  81.6 us (24%)
  waiting for transfers between devices  56.8 us (17%)
  local copies, waits for them, and re-layouts  46.9 us (14%)
  other arithmetic  32.9 us (10%)
  between operations  14.9 us (4%)
    pallas_call x1, Pallas kernels, weight_grads(): pl.pallas_call(weight_grads_kernel, out_shape=(jax.ShapeDtypeStruct((8, 3...  81.6 us
    all_gather x1, waiting for transfers between devices, on_device(): lax.all_gather(keys, 'blk', axis=1, tiled=True)  23.5 us
    reduce_scatter x1, waiting for transfers between devices, on_device(): lax.psum_scatter(jnp.concatenate((key_term, value_term), axis=2).reshape(...  20.7 us
    unnamed x132, local copies, waits for them, and re-layouts  16.6 us
    dot_general x1, matrix products, on_device(): jnp.einsum('td,fd->tf', upstream_b, fc2_weight, preferred_element_type=jn...  13.7 us
    all_gather x1, waiting for transfers between devices, on_device(): lax.all_gather(values, 'blk', axis=1, tiled=True)  12.6 us
    dot_general x4, matrix products, on_device(): jnp.einsum('td,pd->tp', stream_grad_b, emb_weight[band_index], preferred_...  12.6 us
    convert_element_type x1, other arithmetic, on_device(): score_grad_b = (probs * (prob_grad - jnp.sum(probs * prob_grad, axis=-1,...  11.8 us
  transfers between devices with their start and end apart: 3, of which 3 were waited for; matrix products, arithmetic and copies ran while one was open for 14% of the time, Pallas kernels for 0%

profile of v1, /device:TPU:0, one launch (start us, length us, event | category | flops | bytes accessed | tf_op | source)
XLA Modules:
  0.0 336.0 jit_solution(11614732193845988338)
XLA Ops:
  7.3 1.6 fusion.106
  9.3 2.3 fusion.60
  11.5 2.1 fusion.57
  16.6 0.8 slice-done.5
  17.4 1.8 fusion.123
  19.3 1.7 copy-done.17
  20.9 0.9 slice.198
  21.9 2.8 fusion.97
  25.3 2.0 copy.51
  27.6 23.5 %all-gather.7.cloned.1.call-done = bf16[1024,1024]{1,0:T(8,128)(2,1)} async-done(((bf16[256,1024]{1,0:T(8,128)(2,1)}), bf16[1024,1024]{1,0:T(8,128)(2,1)}) %all-gather.7.cloned.1.call-update) | async-done | bytes 2097168 | tf_op jit(solution)/shard_map/all_gather | solution.py:435
  51.1 3.9 %copy.52 = bf16[1024,1024]{0,1:T(8,128)(2,1)} copy(bf16[1024,1024]{1,0:T(8,128)(2,1)} %all-gather.7.cloned.1.call-done) | data formatting | bytes 4194304 | tf_op jit(solution)/shard_map/all_gather | solution.py:435
  55.0 5.0 %fusion.121 = (f32[16,256]{1,0:T(8,128)S(1)}, f32[16,256,1024]{2,1,0:T(8,128)S(1)}) fusion(bf16[256,16,64]{0,2,1:T(8,128)(2,1)} %bitcast.160, bf16[1024,16,64]{0,2,1:T(8,128)(2,1)} %bitcast.155, pred[256,1024]{1,0:T(8,128)(4,1)S(1)} %broadcast_compare_fusion), kind=kOutput, calls=%fused_computation.154 | convolution fusion | flops 549449728 | bytes 19677184 | tf_op jit(solution)/shard_map/rqhd,rkhd->rhqk/dot_general | solution.py:429
  60.0 3.8 %fusion = f32[16,256]{1,0:T(8,128)S(1)} fusion(f32[16,256,1024]{2,1,0:T(8,128)S(1)} %get-tuple-element.103, f32[16,256]{1,0:T(8,128)S(1)} %get-tuple-element.102), kind=kLoop, calls=%fused_computation.6 | loop fusion | flops 8384512 | bytes 16809984 | tf_op jit(solution)/shard_map/reduce_sum | solution.py:441
  63.8 2.4 copy-done.1
  66.2 12.6 %all-gather.5.cloned.1.call-done = bf16[1024,1024]{1,0:T(8,128)(2,1)} async-done(((bf16[256,1024]{1,0:T(8,128)(2,1)}), bf16[1024,1024]{1,0:T(8,128)(2,1)}) %all-gather.5.cloned.1.call-update) | async-done | bytes 2097168 | tf_op jit(solution)/shard_map/all_gather | solution.py:436
  78.8 4.0 %copy.50 = bf16[1024,1024]{0,1:T(8,128)(2,1)} copy(bf16[1024,1024]{1,0:T(8,128)(2,1)} %all-gather.5.cloned.1.call-done) | data formatting | bytes 4194304 | tf_op jit(solution)/shard_map/all_gather | solution.py:436
  82.8 8.2 %fusion.89 = bf16[16,64,256]{2,1,0:T(8,128)(2,1)S(1)} fusion(bf16[1024,16,64]{0,2,1:T(8,128)(2,1)} %bitcast.158, f32[16,256,1024]{2,1,0:T(8,128)} %copy-done.1, f32[16,256]{1,0:T(8,128)S(1)} %fusion, f32[16,256]{1,0:T(8,128)S(1)} %get-tuple-element.102), kind=kOutput, calls=%fused_computation.86 | convolution fusion | flops 549715968 | bytes 19431424 | tf_op jit(solution)/shard_map/rhqk,rkhd->rqhd/dot_general | solution.py:444
  92.7 6.5 %convolution_add_fusion = f32[256,4096]{1,0:T(8,128)S(1)} fusion(bf16[256,1024]{1,0:T(8,128)(2,1)S(1)} %get-tuple-element.110.n2_in, bf16[1024,4096]{1,0:T(8,128)(2,1)} %param.36, f32[4096]{0:T(1024)S(1)} %copy-done.55), kind=kOutput, calls=%fused_computation.12 | convolution fusion | flops 2148532224 | bytes 13123584 | tf_op jit(solution)/shard_map/dot_general | solution.py:455
  99.3 13.7 %convert_reduce_fusion = (f32[4096]{0:T(1024)S(1)}, bf16[256,4096]{1,0:T(8,128)(2,1)S(1)}, f32[256,4096]{1,0:T(8,128)}) fusion(f32[256,4096]{1,0:T(8,128)S(1)} %convolution_add_fusion, bf16[256,1024]{1,0:T(8,128)(2,1)S(1)} %get-tuple-element.85.gout_in, bf16[4096,1024]{1,0:T(8,128)(2,1)S(1)} %bitcast.193), kind=kOutput, calls=%fused_computation.15 | convolution fusion | flops 2225074176 | bytes 19415040 | tf_op jit(solution)/shard_map/td,fd->tf/dot_general | solution.py:466
  113.0 2.7 multiply_reduce_fusion.1
  116.1 1.0 copy-done.5
  118.2 1.5 convolution_convert_fusion
  119.7 2.0 copy.53
  121.7 8.8 %convert_bitcast_fusion = bf16[1024,1,16,64]{0,3,2,1:T(8,128)(2,1)S(1)} fusion(bf16[256,16,64]{0,2,1:T(8,128)(2,1)} %bitcast.162, f32[16,256,1024]{2,1,0:T(8,128)} %copy-done.1, f32[16,256]{1,0:T(8,128)S(1)} %log_add_fusion), kind=kOutput, calls=%fused_computation.32 | convolution fusion | flops 546308096 | bytes 19415040 | tf_op jit(solution)/shard_map/rhqk,rqhd->krhd/dot_general | solution.py:504
  130.6 11.1 %multiply_reduce_fusion = (f32[16,256]{1,0:T(8,128)S(1)}, f32[16,256,1024]{2,1,0:T(8,128)}) fusion(f32[16,256,1024]{2,1,0:T(8,128)} %copy-done.1, f32[16,256]{1,0:T(8,128)S(1)} %log_add_fusion, bf16[256,16,64]{0,2,1:T(8,128)(2,1)S(1)} %bitcast.163, bf16[1024,16,64]{0,2,1:T(8,128)(2,1)S(1)} %bitcast.159), kind=kOutput, calls=%fused_computation.1 | convolution fusion | flops 549449728 | bytes 36208640 | tf_op jit(solution)/shard_map/rqhd,rkhd->rhqk/dot_general | solution.py:488
  141.7 11.8 %multiply_convert_fusion = bf16[16,256,1024]{2,1,0:T(8,128)(2,1)S(1)} fusion(f32[16,256,1024]{2,1,0:T(8,128)} %get-tuple-element.108, f32[16,256,1024]{2,1,0:T(8,128)} %copy-done.1, f32[16,256]{1,0:T(8,128)S(1)} %get-tuple-element.107, f32[16,256]{1,0:T(8,128)S(1)} %log_add_fusion), kind=kLoop, calls=%fused_computation | loop fusion | flops 16777216 | bytes 41975808 | tf_op jit(solution)/shard_map/convert_element_type | solution.py:493
  153.5 3.2 copy-done.2
  156.7 1.6 fusion.14
  158.3 2.3 pad_maximum_fusion
  160.6 6.6 %copy.54 = bf16[1024,1,2048]{2,0,1:T(8,128)(2,1)} copy(bf16[1024,1,2048]{0,2,1:T(8,128)(2,1)} %bitcast.157) | data formatting | bytes 8388608 | tf_op jit(solution)/shard_map/convert_element_type | solution.py:510
  168.8 2.0 copy.57.att_in
  171.9 1.1 reshape.316
  173.0 8.5 %fusion.67 = bf16[16,64,256]{2,1,0:T(8,128)(2,1)} fusion(bf16[1024,16,64]{0,2,1:T(8,128)(2,1)} %bitcast.156, bf16[16,256,1024]{2,1,0:T(8,128)(2,1)} %copy-done.2), kind=kOutput, calls=%fused_computation.78 | convolution fusion | flops 537395200 | bytes 11010048 | tf_op jit(solution)/shard_map/rhqk,rkhd->rqhd/dot_general | solution.py:495
  181.5 2.0 copy.55
  183.5 1.2 convert_reduce_fusion.4
  184.8 4.3 %multiply_convert_fusion.2.hid_in = bf16[256,4096]{1,0:T(8,128)(2,1)S(1)} fusion(f32[256,4096]{1,0:T(8,128)} %get-tuple-element.83, f32[256,4096]{1,0:T(8,128)} %copy-done.15), kind=kLoop, calls=%fused_computation.18 | loop fusion | flops 3145728 | bytes 10485760 | tf_op jit(solution)/shard_map/convert_element_type | solution.py:456
  189.1 1.3 copy-done.8
  190.4 7.2 %fusion.93 = bf16[1,256,1024]{2,1,0:T(8,128)(2,1)} fusion(f32[256,1024]{1,0:T(8,128)S(1)} %copy-done.4, bf16[256,4096]{1,0:T(8,128)(2,1)S(1)} %multiply_convert_fusion.2.hid_in, bf16[4096,1024]{1,0:T(8,128)(2,1)} %param.38, f32[1024]{0:T(1024)S(1)} %copy-done.56, f32[256]{0:T(256)S(1)} %bitcast.175), kind=kOutput, calls=%fused_computation.88 | convolution fusion | flops 2148532224 | bytes 12063744 | tf_op jit(solution)/shard_map/dot_general | solution.py:457
  197.6 20.7 %reduce-scatter.2.cloned.1.call-done = bf16[256,1,2048]{2,0,1:T(8,128)(2,1)} async-done(((bf16[1024,1,2048]{2,0,1:T(8,128)(2,1)}), bf16[256,1,2048]{2,0,1:T(8,128)(2,1)}) %reduce-scatter.2.cloned.1.call-update) | async-done | bytes 1048592 | tf_op jit(solution)/shard_map/reduce_scatter | solution.py:507
  218.3 1.1 convert_reduce_fusion.3
  219.5 5.5 %multiply_reduce_fusion.2 = (f32[1024]{0:T(1024)S(1)}, f32[256]{0:T(256)S(1)}, f32[1024]{0:T(1024)S(1)}, f32[256,1024]{1,0:T(8,128)S(1)}) fusion(f32[256,1024]{1,0:T(8,128)S(1)} %get-tuple-element.101, f32[256]{0:T(256)S(1)} %fusion.107, f32[256]{0:T(256)S(1)} %broadcast_multiply_fusion.1, f32[1024]{0:T(1024)S(1)} %copy-done.36, ...), kind=kOutput, calls=%fused_computation.103 | convolution fusion | flops 1615853312 | bytes 9976832 | tf_op jit(solution)/shard_map/te,de->td/dot_general | solution.py:521
  225.0 1.3 pad_maximum_fusion.1.gp_in
  227.5 1.3 concatenate.13.row_in
  228.8 81.6 %weight_grads.1 = (f32[8,3072]{1,0:T(8,128)}, f32[8,3072]{1,0:T(8,128)}, f32[8,1024]{1,0:T(8,128)}, f32[8,4096]{1,0:T(8,128)}, f32[32,1024]{1,0:T(8,128)}, /*index=5*/f32[8,128]{1,0:T(8,128)}) custom-call(bf16[256,1024]{1,0:T(8,128)(2,1)} %copy-done.9, bf16[256,768]{1,0:T(8,128)(2,1)} %bitcast.170, bf16[256,128]{1,0:T(8,128)(2,1)} %pad.5.hot_in, ...), custom_call_target="tpu_custom_call" | custom-call | tf_op jit(solution)/shard_map/weight_grads/pallas_call | solution.py:314
  312.0 3.1 fusion.86
  315.1 3.1 fusion.83
  318.3 3.0 fusion.80
  322.6 3.5 %fusion.94 = bf16[1,256,768]{2,1,0:T(8,128)(2,1)} fusion(f32[256,768]{1,0:T(8,128)} %fusion.86, f32[256,768]{1,0:T(8,128)} %fusion.83, f32[256,768]{1,0:T(8,128)} %fusion.80, bf16[256,1024]{1,0:T(8,128)(2,1)S(1)} %copy-done.10, bf16[4,768,1024]{2,1,0:T(8,128)(2,1)} %param.25, f32[256]{0:T(256)S(1)} %copy-done.43), kind=kOutput, calls=%fused_computation.89 | convolution fusion | flops 403636224 | bytes 4850688 | tf_op jit(solution)/shard_map/td,pd->tp/dot_general | solution.py:530
  (168 shorter events, 17.1 us)
Async XLA Ops:
  7.2 83.9 %copy-start = (bf16[1024,1024]{1,0:T(8,128)(2,1)S(1)}, bf16[1024,1024]{1,0:T(8,128)(2,1)}, u32[]{:S(2)}) copy-start(bf16[1024,1024]{1,0:T(8,128)(2,1)} %param.32) | copy-start | bytes 6291460
  7.2 6.4 %copy-start.25 = (bf16[1,256,768]{2,1,0:T(8,128)(2,1)S(1)}, bf16[1,256,768]{2,1,0:T(8,128)(2,1)}, u32[]{:S(2)}) copy-start(bf16[1,256,768]{2,1,0:T(8,128)(2,1)} %param.20) | copy-start | bytes 1179652
  7.2 43.8 %all-gather.7.cloned.1.call-start = ((), (), s32[]{:S(2)}) async-start(), calls=%async_computation.3 | async-start | bytes 2621440 | tf_op jit(solution)/shard_map/all_gather | solution.py:435
  7.3 6.4 %copy-start.26 = (bf16[4,768,1024]{2,1,0:T(8,128)(2,1)S(1)}, bf16[4,768,1024]{2,1,0:T(8,128)(2,1)}, u32[]{:S(2)}) copy-start(bf16[4,768,1024]{2,1,0:T(8,128)(2,1)} %param.25) | copy-start | bytes 18874372
  9.2 5.1 %copy-start.49 = (f32[256]{0:T(256)}, f32[256]{0:T(256)S(1)}, u32[]{:S(2)}) copy-start(f32[256]{0:T(256)S(1)} %get-tuple-element.72) | copy-start | bytes 3076
  9.2 5.1 %copy-start.51 = (f32[256]{0:T(256)}, f32[256]{0:T(256)S(1)}, u32[]{:S(2)}) copy-start(f32[256]{0:T(256)S(1)} %get-tuple-element.71) | copy-start | bytes 3076
  9.2 5.1 %copy-start.53 = (f32[256]{0:T(256)}, f32[256]{0:T(256)S(1)}, u32[]{:S(2)}) copy-start(f32[256]{0:T(256)S(1)} %get-tuple-element.70) | copy-start | bytes 3076
  9.2 5.8 %copy-start.42 = (f32[256]{0:T(256)}, f32[256]{0:T(256)S(1)}, u32[]{:S(2)}) copy-start(f32[256]{0:T(256)S(1)} %get-tuple-element.69) | copy-start | bytes 3076
  9.2 5.1 %copy-start.27 = (bf16[1,256,1024]{2,1,0:T(8,128)(2,1)S(1)}, bf16[1,256,1024]{2,1,0:T(8,128)(2,1)}, u32[]{:S(2)}) copy-start(bf16[1,256,1024]{2,1,0:T(8,128)(2,1)} %param.21) | copy-start | bytes 1572868
  9.2 5.1 %copy-start.34 = (f32[4,1024]{1,0:T(4,128)S(1)}, f32[4,1024]{1,0:T(4,128)}, u32[]{:S(2)}) copy-start(f32[4,1024]{1,0:T(4,128)} %param.26) | copy-start | bytes 49156
  9.2 5.1 %copy-start.38 = (s32[1,256]{1,0:T(1,128)S(1)}, s32[1,256]{1,0:T(1,128)}, u32[]{:S(2)}) copy-start(s32[1,256]{1,0:T(1,128)} %param.23) | copy-start | bytes 3076
  15.0 2.4 slice-start.5
  16.1 3.1 copy-start.40
  17.4 4.5 %copy-start.46 = (f32[1024]{0:T(1024)S(1)}, f32[1024]{0:T(1024)}, u32[]{:S(2)}) copy-start(f32[1024]{0:T(1024)} %param.30) | copy-start | bytes 12292
  17.4 4.5 %copy-start.47 = (f32[1024]{0:T(1024)S(1)}, f32[1024]{0:T(1024)}, u32[]{:S(2)}) copy-start(f32[1024]{0:T(1024)} %param.31) | copy-start | bytes 12292
  20.9 6.4 %copy-start.44 = (s32[1,1024]{1,0:T(1,128)S(1)}, s32[1,1024]{1,0:T(1,128)}, u32[]{:S(2)}) copy-start(s32[1,1024]{1,0:T(1,128)} %param.22) | copy-start | bytes 12292
  21.8 57.0 %all-gather.5.cloned.1.call-start = ((), (), s32[]{:S(2)}) async-start(), calls=%async_computation.2 | async-start | bytes 2621440 | tf_op jit(solution)/shard_map/all_gather | solution.py:436
  24.7 193.6 %reduce-scatter.2.cloned.1.call-start = ((), (), s32[]{:S(2)}) async-start(), calls=%async_computation.1 | async-start | bytes 5242880 | tf_op jit(solution)/shard_map/reduce_scatter | solution.py:507
  60.0 6.2 %copy-start.1 = (f32[16,256,1024]{2,1,0:T(8,128)}, f32[16,256,1024]{2,1,0:T(8,128)S(1)}, u32[]{:S(2)}) copy-start(f32[16,256,1024]{2,1,0:T(8,128)S(1)} %get-tuple-element.103) | copy-start | bytes 50331652
  82.8 8.3 %copy-start.37 = (f32[1024]{0:T(1024)S(1)}, f32[1024]{0:T(1024)}, u32[]{:S(2)}) copy-start(f32[1024]{0:T(1024)} %param.33) | copy-start | bytes 12292
  91.1 8.2 %slice-start.2 = ((s8[8388608]{0:T(1024)(128)(4,1)}), s8[4194304]{0:T(1024)(128)(4,1)S(1)}, s32[]{:S(2)}) async-start(s8[8388608]{0:T(1024)(128)(4,1)} %bitcast.192), calls=%async_computation.6 | async-start | bytes 8388608
  91.9 23.8 %copy-start.3 = (f32[256,1024]{1,0:T(8,128)}, f32[256,1024]{1,0:T(8,128)S(1)}, u32[]{:S(2)}) copy-start(f32[256,1024]{1,0:T(8,128)S(1)} %get-tuple-element.105) | copy-start | bytes 3145732
  92.7 6.6 %copy-start.21 = (bf16[256,1024]{1,0:T(8,128)(2,1)}, bf16[256,1024]{1,0:T(8,128)(2,1)S(1)}, u32[]{:S(2)}) copy-start(bf16[256,1024]{1,0:T(8,128)(2,1)S(1)} %get-tuple-element.110.n2_in) | copy-start | bytes 1572868
  92.7 6.6 %copy-start.20 = (bf16[256,1024]{1,0:T(8,128)(2,1)}, bf16[256,1024]{1,0:T(8,128)(2,1)S(1)}, u32[]{:S(2)}) copy-start(bf16[256,1024]{1,0:T(8,128)(2,1)S(1)} %get-tuple-element.85.gout_in) | copy-start | bytes 1572868
  92.7 6.6 %slice-start.3 = ((s8[8388608]{0:T(1024)(128)(4,1)}), s8[4194304]{0:T(1024)(128)(4,1)S(1)}, s32[]{:S(2)}) async-start(s8[8388608]{0:T(1024)(128)(4,1)} %bitcast.192), calls=%async_computation.7 | async-start | bytes 8388608
  92.7 20.3 %slice-start = ((s8[8388608]{0:T(1024)(128)(4,1)}), s8[4194304]{0:T(1024)(128)(4,1)S(1)}, s32[]{:S(2)}) async-start(s8[8388608]{0:T(1024)(128)(4,1)} %bitcast.190), calls=%async_computation.4 | async-start | bytes 8388608
  99.2 13.7 %copy-start.15 = (f32[256,4096]{1,0:T(8,128)}, f32[256,4096]{1,0:T(8,128)S(1)}, u32[]{:S(2)}) copy-start(f32[256,4096]{1,0:T(8,128)S(1)} %convolution_add_fusion) | copy-start | bytes 12582916
  99.3 13.7 %slice-start.1 = ((s8[8388608]{0:T(1024)(128)(4,1)}), s8[4194304]{0:T(1024)(128)(4,1)S(1)}, s32[]{:S(2)}) async-start(s8[8388608]{0:T(1024)(128)(4,1)} %bitcast.190), calls=%async_computation.5 | async-start | bytes 8388608
  113.0 2.7 copy-start.23
  121.7 8.8 %copy-start.7 = (bf16[1024,1024]{0,1:T(8,128)(2,1)S(1)}, bf16[1024,1024]{0,1:T(8,128)(2,1)}, u32[]{:S(2)}) copy-start(bf16[1024,1024]{0,1:T(8,128)(2,1)} %copy.50) | copy-start | bytes 6291460
  121.7 8.8 %copy-start.12 = (bf16[256,1024]{0,1:T(8,128)(2,1)S(1)}, bf16[256,1024]{0,1:T(8,128)(2,1)}, u32[]{:S(2)}) copy-start(bf16[256,1024]{0,1:T(8,128)(2,1)} %copy.53) | copy-start | bytes 1572868
  141.7 15.0 %copy-start.11 = (bf16[256,1024]{0,1:T(8,128)(2,1)S(1)}, bf16[256,1024]{0,1:T(8,128)(2,1)}, u32[]{:S(2)}) copy-start(bf16[256,1024]{0,1:T(8,128)(2,1)} %copy.51) | copy-start | bytes 1572868
  153.5 3.2 copy-start.2
  184.8 5.6 %copy-start.4 = (f32[256,1024]{1,0:T(8,128)S(1)}, f32[256,1024]{1,0:T(8,128)}, u32[]{:S(2)}) copy-start(f32[256,1024]{1,0:T(8,128)} %copy-done.3) | copy-start | bytes 3145732
  184.8 5.6 %copy-start.56 = (f32[1024]{0:T(1024)S(1)}, f32[1024]{0:T(1024)}, u32[]{:S(2)}) copy-start(f32[1024]{0:T(1024)} %param.39) | copy-start | bytes 12292
  219.4 5.5 %copy-start.16 = (bf16[256,1,2048]{2,0,1:T(8,128)(2,1)S(1)}, bf16[256,1,2048]{2,0,1:T(8,128)(2,1)}, u32[]{:S(2)}) copy-start(bf16[256,1,2048]{2,0,1:T(8,128)(2,1)} %reduce-scatter.2.cloned.1.call-done) | copy-start | bytes 3145732
  219.4 5.5 %copy-start.22 = (bf16[256,1024]{1,0:T(8,128)(2,1)S(1)}, bf16[256,1024]{1,0:T(8,128)(2,1)}, u32[]{:S(2)}) copy-start(bf16[256,1024]{1,0:T(8,128)(2,1)} %copy.55) | copy-start | bytes 1572868
  219.5 6.8 %copy-start.41 = (f32[256]{0:T(256)S(1)}, f32[256]{0:T(256)}, u32[]{:S(2)}) copy-start(f32[256]{0:T(256)} %copy-done.40) | copy-start | bytes 3076
  228.8 83.2 %copy-start.54 = (f32[256]{0:T(256)S(1)}, f32[256]{0:T(256)}, u32[]{:S(2)}) copy-start(f32[256]{0:T(256)} %copy-done.53) | copy-start | bytes 3076
  228.8 86.3 %copy-start.52 = (f32[256]{0:T(256)S(1)}, f32[256]{0:T(256)}, u32[]{:S(2)}) copy-start(f32[256]{0:T(256)} %copy-done.51) | copy-start | bytes 3076
  310.4 7.8 %copy-start.10 = (bf16[256,1024]{1,0:T(8,128)(2,1)S(1)}, bf16[256,1024]{1,0:T(8,128)(2,1)}, u32[]{:S(2)}) copy-start(bf16[256,1024]{1,0:T(8,128)(2,1)} %copy-done.9) | copy-start | bytes 1572868
  310.4 7.8 %copy-start.50 = (f32[256]{0:T(256)S(1)}, f32[256]{0:T(256)}, u32[]{:S(2)}) copy-start(f32[256]{0:T(256)} %copy-done.49) | copy-start | bytes 3076
  315.1 7.5 %copy-start.43 = (f32[256]{0:T(256)S(1)}, f32[256]{0:T(256)}, u32[]{:S(2)}) copy-start(f32[256]{0:T(256)} %copy-done.42) | copy-start | bytes 3076
  318.2 7.8 %copy-start.32 = (f32[8,3072]{1,0:T(8,128)S(1)}, f32[8,3072]{1,0:T(8,128)}, u32[]{:S(2)}) copy-start(f32[8,3072]{1,0:T(8,128)} %get-tuple-element.23) | copy-start | bytes 294916
  318.2 8.5 %copy-start.31 = (f32[8,3072]{1,0:T(8,128)S(1)}, f32[8,3072]{1,0:T(8,128)}, u32[]{:S(2)}) copy-start(f32[8,3072]{1,0:T(8,128)} %get-tuple-element.134) | copy-start | bytes 294916
  318.2 9.1 %copy-start.33 = (f32[8,1024]{1,0:T(8,128)S(1)}, f32[8,1024]{1,0:T(8,128)}, u32[]{:S(2)}) copy-start(f32[8,1024]{1,0:T(8,128)} %get-tuple-element.137) | copy-start | bytes 98308
  318.2 9.7 %copy-start.30 = (f32[8,4096]{1,0:T(8,128)S(1)}, f32[8,4096]{1,0:T(8,128)}, u32[]{:S(2)}) copy-start(f32[8,4096]{1,0:T(8,128)} %get-tuple-element.141) | copy-start | bytes 393220
  318.2 10.3 %copy-start.29 = (f32[32,1024]{1,0:T(8,128)S(1)}, f32[32,1024]{1,0:T(8,128)}, u32[]{:S(2)}) copy-start(f32[32,1024]{1,0:T(8,128)} %get-tuple-element.143) | copy-start | bytes 393220
  (18 other events, 26.4 us)
Sparse Core Ops, SparseCore 0:
  22.0 29.0 all-gather.6
  52.7 26.0 all-gather.4
  167.4 50.8 reduce-scatter.1
